TPU v7x, 512 devices: a whole 4x4x16 slice. The times are simulated.
512 devices in a mesh: row: 32 (over y, x, core), col: 16 (over z).
Axes of the slice: x: 4, y: 4, z: 16, core: 2. Of those that a mesh axis runs over, the one named last changes fastest.
Arguments:
- col_samples: float32 [64, 2, 2048, 128], P('row', None, 'col'), may hold values from -6 to 6
- row_samples: float32 [64, 2, 128, 2048], P('row', None, None, 'col'), may hold values from -6 to 6
- pivot_rows: int32 [64, 128], P('row'), may hold values from 0 to 2047
- rank_blocks: int32 [64], P('row'), may hold values from 1 to 8
- upper_inverse: float32 [2, 2048, 2048], P(None, 'col', 'row'), as said below
- upanel_left: float32 [16, 2, 2048, 128], P('col'), may hold values from -0.125 to 0.125
Outputs:
- panel_right: float32 [64, 2, 128, 2048], P('row', None, None, 'col')
- cores: float32 [64, 16, 2, 128, 128], P('row', 'col')
Inputs may be any that keep to these rules, and one draw needn't show every extreme that they name: `rank_blocks`: the tile's rank is 16 times this. `upper_inverse`: zero below the diagonal in both parts.
All inputs are finite; a program needn't handle non-finite values.
Results may differ from a plain program's by a relative error of at most 0.00007.
Values sent between devices are 32-bit elements; how exact they have to be, the bound alone decides.
No kernel may reach another device: no remote copies, remote signals or barrier semaphores. Data moves between devices by JAX's collectives and lax.ppermute only.
A program may use at most 64 MiB of HBM per device.

v0:
```python
import jax
import jax.numpy as jnp
from jax import lax
from jax.sharding import PartitionSpec as P

RANK_STEP = 16


def complex_product(pattern, left_real, left_imag, right_real, right_imag):

    def single(left, right):
        return jnp.einsum(
            pattern,
            left,
            right,
            precision=lax.Precision.HIGHEST,
            preferred_element_type=jnp.float32,
        )

    real_part = single(left_real, right_real) - single(left_imag, right_imag)
    imag_part = single(left_real, right_imag) + single(left_imag, right_real)
    return (real_part, imag_part)


def scale_rows(values, weight_real, weight_imag):
    wr = weight_real[:, :, None]
    wi = weight_imag[:, :, None]
    real_part = values[:, 0] * wr - values[:, 1] * wi
    imag_part = values[:, 0] * wi + values[:, 1] * wr
    return jnp.stack((real_part, imag_part), axis=1)


def on_device(col_samples, row_samples, pivot_rows, rank_blocks, upper_inverse, upanel_left):
    width_local = col_samples.shape[2]
    ranks_max = row_samples.shape[2]
    offset = lax.axis_index("col") * width_local
    positions = offset + lax.broadcasted_iota(jnp.int32, (1, 1, width_local), 2)
    hits = (pivot_rows[:, :, None] == positions).astype(jnp.float32)
    flipped = jnp.swapaxes(col_samples, 2, 3)
    partial_entries = jnp.sum(flipped * hits[:, None], axis=3)
    entries = lax.psum(partial_entries, "col")
    levels = lax.broadcasted_iota(jnp.int32, (1, ranks_max), 1)
    keeping = (levels < RANK_STEP * rank_blocks[:, None]).astype(jnp.float32)
    magnitude = jnp.maximum(entries[:, 0] * entries[:, 0] + entries[:, 1] * entries[:, 1], 1.0)
    factor_real = keeping * entries[:, 0] / magnitude
    factor_imag = -keeping * entries[:, 1] / magnitude
    scaled = scale_rows(row_samples, factor_real, factor_imag)
    portion = lax.all_gather(upper_inverse, "row", axis=2, tiled=True)
    real_part, imag_part = complex_product(
        "trk,kn->trn", scaled[:, 0], scaled[:, 1], portion[0], portion[1]
    )
    partial_panel = jnp.stack((real_part, imag_part), axis=1)
    panel_local = lax.psum_scatter(partial_panel, "col", scatter_dimension=3, tiled=True)
    portion = lax.all_gather(panel_local, "col", axis=3, tiled=True)
    core_real, core_imag = complex_product(
        "trn,jns->tjrs", portion[:, 0], portion[:, 1], upanel_left[:, 0], upanel_left[:, 1]
    )
    cores = jnp.stack((core_real, core_imag), axis=2)
    return (panel_local, cores)


def solution(mesh):
    in_specs = (
        P("row", None, "col", None),
        P("row", None, None, "col"),
        P("row", None),
        P("row"),
        P(None, "col", "row"),
        P("col", None, None, None),
    )
    out_specs = (P("row", None, None, "col"), P("row", "col", None, None, None))
    return jax.shard_map(
        on_device, mesh=mesh, in_specs=in_specs, out_specs=out_specs, check_vma=False
    )
```

profile of v0, /device:TPU:2, one launch (start us, length us, event | category | flops | bytes accessed | tf_op | source)
XLA Modules:
  0.0 281.9 jit_solution(7301261295972462733)
XLA Ops:
  7.2 0.0 all-gather.3.cloned.1.call-start
  7.2 1.5 copy.12
  8.7 0.0 all-gather.3.cloned.1.call-update
  8.8 0.0 reduce-scatter.2.cloned.1.call-start
  8.8 0.8 compare_convert_fusion
  9.6 1.0 fusion.18
  10.6 36.5 %psum.7 = f32[2,2,128]{2,1,0:T(2,128)S(1)} all-reduce(f32[2,2,128]{2,1,0:T(2,128)S(1)} %fusion.18), channel_id=1, replica_groups=mesh['row'=32,'col'=16] {'col'}, use_global_device_ids=true, to_apply=%region_1.0 | all-reduce | flops 512 | bytes 4096 | tf_op jit(solution)/shard_map/psum | solution.py:41
  47.1 0.7 broadcast_multiply_fusion
  47.8 0.1 select_divide_fusion
  47.8 0.0 copy-start.2
  47.8 27.1 %all-gather.3.cloned.1.call-done = f32[2,128,2048]{1,0,2:T(2,128)} async-done(((f32[2,128,64]{1,0,2:T(2,128)}), f32[2,128,2048]{1,0,2:T(2,128)}) %all-gather.3.cloned.1.call-update) | async-done | bytes 2097168 | tf_op jit(solution)/shard_map/all_gather | solution.py:48
  74.9 4.0 %fusion.25 = (f32[1,128,2048]{1,0,2:T(1,128)S(1)}, f32[1,128,2048]{1,0,2:T(1,128)S(1)}) fusion(f32[2,128,2048]{1,0,2:T(2,128)} %all-gather.3.cloned.1.call-done), kind=kLoop, calls=%fused_computation.41 | loop fusion | bytes 4194304 | tf_op jit(solution)/shard_map/slice | solution.py:50
  78.9 0.0 copy-done.2
  78.9 1.8 fusion.21
  80.8 1.8 fusion.23
  82.6 1.9 fusion
  84.5 1.9 fusion.1
  86.4 2.2 pad_maximum_fusion
  88.6 0.0 copy-start.1
  88.6 0.0 reduce-scatter.2.cloned.1.call-update
  88.7 0.2 all-gather.5.cloned.1.call-start
  88.9 79.6 %reduce-scatter.2.cloned.1.call-done = f32[2,2,128,128]{3,2,0,1:T(8,128)} async-done(((f32[2,2,128,2048]{3,2,0,1:T(8,128)}), f32[2,2,128,128]{3,2,0,1:T(8,128)}) %reduce-scatter.2.cloned.1.call-update) | async-done | bytes 262160 | tf_op jit(solution)/shard_map/reduce_scatter | solution.py:53
  168.5 0.0 all-gather.5.cloned.1.call-update
  168.5 1.7 copy.15
  170.2 93.8 %all-gather.5.cloned.1.call-done = f32[2,2,128,2048]{3,2,0,1:T(8,128)} async-done(((f32[2,2,128,128]{3,2,0,1:T(8,128)}), f32[2,2,128,2048]{3,2,0,1:T(8,128)}) %all-gather.5.cloned.1.call-update) | async-done | bytes 4194320 | tf_op jit(solution)/shard_map/all_gather | solution.py:54
  263.9 0.0 copy-done.1
  263.9 0.0 copy-start
  263.9 3.6 %fusion.2 = f32[2,128,128]{2,1,0:T(8,128)S(1)} fusion(f32[2,2,128,2048]{3,2,0,1:T(8,128)} %all-gather.5.cloned.1.call-done, f32[1,2,2048,128]{3,2,1,0:T(8,128)S(1)} %copy-done.1), kind=kOutput, calls=%fused_computation.7 | convolution fusion | flops 805306368 | bytes 3276800 | tf_op jit(solution)/shard_map/trn,jns->tjrs/dot_general | solution.py:12
  267.5 3.4 %fusion.3 = f32[2,128,128]{2,1,0:T(8,128)S(1)} fusion(f32[2,2,128,2048]{3,2,0,1:T(8,128)} %all-gather.5.cloned.1.call-done, f32[1,2,2048,128]{3,2,1,0:T(8,128)S(1)} %copy-done.1), kind=kOutput, calls=%fused_computation.8 | convolution fusion | flops 805306368 | bytes 3276800 | tf_op jit(solution)/shard_map/trn,jns->tjrs/dot_general | solution.py:12
  270.9 0.0 copy-done
  270.9 1.8 fusion.9
  272.8 1.8 fusion.7
  274.6 0.7 copy.16
  (3 shorter events, 0.0 us)
Async XLA Ops:
  7.2 67.7 %all-gather.3.cloned.1.call-start = ((), (), s32[]{:S(2)}) async-start(), calls=%async_computation.1 | async-start | bytes 2162688 | tf_op jit(solution)/shard_map/all_gather | solution.py:48
  8.8 159.7 %reduce-scatter.2.cloned.1.call-start = ((), (), s32[]{:S(2)}) async-start(), calls=%async_computation.2 | async-start | bytes 4456448 | tf_op jit(solution)/shard_map/reduce_scatter | solution.py:53
  47.8 31.1 %copy-start.2 = (f32[2,2,128,128]{3,2,1,0:T(8,128)S(1)}, f32[2,2,128,128]{3,2,1,0:T(8,128)}, u32[]{:S(2)}) copy-start(f32[2,2,128,128]{3,2,1,0:T(8,128)} %param.7) | copy-start | bytes 786436
  88.6 175.3 %copy-start.1 = (f32[1,2,2048,128]{3,2,1,0:T(8,128)S(1)}, f32[1,2,2048,128]{3,2,1,0:T(8,128)}, u32[]{:S(2)}) copy-start(f32[1,2,2048,128]{3,2,1,0:T(8,128)} %param.11) | copy-start | bytes 6291460
  88.7 175.3 %all-gather.5.cloned.1.call-start = ((), (), s32[]{:S(2)}) async-start(), calls=%async_computation.3 | async-start | bytes 4456448 | tf_op jit(solution)/shard_map/all_gather | solution.py:54
  263.9 7.0 %copy-start = (f32[2,2,128,2048]{3,2,0,1:T(8,128)S(1)}, f32[2,2,128,2048]{3,2,0,1:T(8,128)}, u32[]{:S(2)}) copy-start(f32[2,2,128,2048]{3,2,0,1:T(8,128)} %all-gather.5.cloned.1.call-done) | copy-start | bytes 12582916
Sparse Core Ops, SparseCore 0:
  11.7 63.1 all-gather.2
  88.8 79.6 reduce-scatter.1
  170.5 93.4 all-gather.4
where the time goes:
time: 282 us
  waiting for transfers between devices  200 us (71%)
  blocking collectives  36.5 us (13%)
  matrix products  18.1 us (6%)
  between operations  13.9 us (5%)
  local copies, waits for them, and re-layouts  7.92 us (3%)
  other arithmetic  4.73 us (2%)
    all_gather x1, waiting for transfers between devices, on_device(): portion = lax.all_gather(panel_local, 'col', axis=3, tiled=True)  93.8 us
    reduce_scatter x1, waiting for transfers between devices, on_device(): lax.psum_scatter(partial_panel, 'col', scatter_dimension=3, tiled=True)  79.6 us
    psum x1, blocking collectives, on_device(): entries = lax.psum(partial_entries, 'col')  36.5 us
    all_gather x1, waiting for transfers between devices, on_device(): portion = lax.all_gather(upper_inverse, 'row', axis=2, tiled=True)  27.1 us
    dot_general x8, matrix products, single(): jnp.einsum(pattern, left, right, precision=lax.Precision.HIGHEST, preferr...  18.1 us
  transfers between devices with their start and end apart: 3, of which 3 were waited for; matrix products, arithmetic and copies ran while one was open for 1% of the time, Pallas kernels for 0%

commit v1 on v0

--- a/solution.py
+++ b/solution.py
@@ -45,7 +45,9 @@
     factor_real = keeping * entries[:, 0] / magnitude
     factor_imag = -keeping * entries[:, 1] / magnitude
     scaled = scale_rows(row_samples, factor_real, factor_imag)
-    portion = lax.all_gather(upper_inverse, "row", axis=2, tiled=True)
+    portion = jnp.concatenate(
+        lax.all_to_all(jnp.stack([upper_inverse] * lax.axis_size("row")), "row", 0, 0), axis=2
+    )
     real_part, imag_part = complex_product(
         "trk,kn->trn", scaled[:, 0], scaled[:, 1], portion[0], portion[1]
     )

time: 282 us -> 255 us (0.904)
  waiting for transfers between devices: 200 us -> 169 us
  starting transfers between devices: 0.3 us -> 9.97 us
    all_gather x1 -> x0, waiting for transfers between devices: 27.1 us -> none  [on_device(): portion = lax.all_gather(upper_inverse, 'row', axis=2, tiled=True)]
    all_to_all x0 -> x1, starting transfers between devices: none -> 9.71 us  [on_device(): lax.all_to_all(jnp.stack([upper_inverse] * lax.axis_size('row')), 'row',...]
    reduce_scatter x1, waiting for transfers between devices: 79.6 us -> 75.7 us  [on_device(): lax.psum_scatter(partial_panel, 'col', scatter_dimension=3, tiled=True)]
    slice x1, local copies, waits for them, and re-layouts: 4 us -> 0.24 us  [on_device(): portion[0]]
  transfers between devices with their start and end apart: 3 -> 3, of which waited for: 3 -> 2; matrix products, arithmetic and copies ran while one was open for 1% -> 1% of each run, Pallas kernels for 0% -> 0%
where the time goes in v1:
time: 255 us
  waiting for transfers between devices  169 us (66%)
  blocking collectives  34.5 us (14%)
  matrix products  18.1 us (7%)
  between operations  14.2 us (6%)
  starting transfers between devices  9.97 us (4%)
  local copies, waits for them, and re-layouts  6.03 us (2%)
    all_gather x1, waiting for transfers between devices, on_device(): portion = lax.all_gather(panel_local, 'col', axis=3, tiled=True)  93.8 us
    reduce_scatter x1, waiting for transfers between devices, on_device(): lax.psum_scatter(partial_panel, 'col', scatter_dimension=3, tiled=True)  75.7 us
    psum x1, blocking collectives, on_device(): entries = lax.psum(partial_entries, 'col')  34.5 us
    dot_general x8, matrix products, single(): jnp.einsum(pattern, left, right, precision=lax.Precision.HIGHEST, preferr...  18.1 us
    all_to_all x1, starting transfers between devices, on_device(): lax.all_to_all(jnp.stack([upper_inverse] * lax.axis_size('row')), 'row',...  9.71 us
  transfers between devices with their start and end apart: 3, of which 2 were waited for; matrix products, arithmetic and copies ran while one was open for 1% of the time, Pallas kernels for 0%

profile of v1, /device:TPU:2, one launch (start us, length us, event | category | flops | bytes accessed | tf_op | source)
XLA Modules:
  0.0 254.7 jit_solution(5950460007113735335)
XLA Ops:
  7.2 2.4 stack.14
  9.6 0.0 copy-start.4
  9.6 0.0 copy-start.3
  9.6 0.0 copy-start.5
  9.6 9.7 %all-to-all-start = ((f32[32,2,128,64]{2,3,1,0:T(8,128)}), f32[32,2,128,64]{2,3,1,0:T(8,128)S(1)}, u32[]{:S(2)}, u32[]{:S(2)}) async-start(f32[32,2,128,64]{2,3,1,0:T(8,128)} %stack.14), calls=%async_computation | async-start | bytes 4194304 | tf_op jit(solution)/shard_map/all_to_all | solution.py:49
  19.3 0.0 reduce-scatter.2.cloned.1.call-start
  19.4 0.0 copy-done.4
  19.4 0.1 compare_convert_fusion
  19.5 0.0 copy-done.3
  19.5 34.5 %psum.7 = f32[2,2,128]{2,1,0:T(2,128)S(1)} all-reduce(f32[2,2,128]{2,1,0:T(2,128)S(1)} %fusion.18), channel_id=1, replica_groups=mesh['row'=32,'col'=16] {'col'}, use_global_device_ids=true, to_apply=%region_1.0 | all-reduce | flops 512 | bytes 4096 | tf_op jit(solution)/shard_map/psum | solution.py:41
  54.1 0.0 copy-done.5
  54.1 0.1 select_divide_fusion
  54.2 0.0 all-to-all-done
  54.2 0.2 copy.35
  54.4 0.0 copy-start.2
  54.4 0.2 fusion.25
  54.7 0.7 copy-done.2
  55.4 1.8 fusion.21
  57.2 1.8 fusion.23
  59.1 1.9 fusion
  61.0 1.9 fusion.1
  62.8 2.2 pad_maximum_fusion
  65.1 0.0 copy-start.1
  65.1 0.0 reduce-scatter.2.cloned.1.call-update
  65.1 0.2 all-gather.2.cloned.1.call-start
  65.3 75.7 %reduce-scatter.2.cloned.1.call-done = f32[2,2,128,128]{3,2,0,1:T(8,128)} async-done(((f32[2,2,128,2048]{3,2,0,1:T(8,128)}), f32[2,2,128,128]{3,2,0,1:T(8,128)}) %reduce-scatter.2.cloned.1.call-update) | async-done | bytes 262160 | tf_op jit(solution)/shard_map/reduce_scatter | solution.py:55
  141.0 0.0 all-gather.2.cloned.1.call-update
  141.0 1.7 copy.23
  142.7 93.8 %all-gather.2.cloned.1.call-done = f32[2,2,128,2048]{3,2,0,1:T(8,128)} async-done(((f32[2,2,128,128]{3,2,0,1:T(8,128)}), f32[2,2,128,2048]{3,2,0,1:T(8,128)}) %all-gather.2.cloned.1.call-update) | async-done | bytes 4194320 | tf_op jit(solution)/shard_map/all_gather | solution.py:56
  236.4 0.0 copy-done.1
  236.4 0.0 copy-start
  236.4 3.5 %fusion.2 = f32[2,128,128]{2,1,0:T(8,128)S(1)} fusion(f32[2,2,128,2048]{3,2,0,1:T(8,128)} %all-gather.2.cloned.1.call-done, f32[1,2,2048,128]{3,2,1,0:T(8,128)S(1)} %copy-done.1), kind=kOutput, calls=%fused_computation.8 | convolution fusion | flops 805306368 | bytes 3276800 | tf_op jit(solution)/shard_map/trn,jns->tjrs/dot_general | solution.py:12
  240.0 3.4 %fusion.3 = f32[2,128,128]{2,1,0:T(8,128)S(1)} fusion(f32[2,2,128,2048]{3,2,0,1:T(8,128)} %all-gather.2.cloned.1.call-done, f32[1,2,2048,128]{3,2,1,0:T(8,128)S(1)} %copy-done.1), kind=kOutput, calls=%fused_computation.9 | convolution fusion | flops 805306368 | bytes 3276800 | tf_op jit(solution)/shard_map/trn,jns->tjrs/dot_general | solution.py:12
  243.4 0.0 copy-done
  243.4 1.8 fusion.9
  245.3 1.8 fusion.7
  247.1 0.7 copy.24
  (5 shorter events, 0.1 us)
Async XLA Ops:
  9.6 9.8 %copy-start.4 = (s32[2,128]{1,0:T(2,128)S(1)}, s32[2,128]{1,0:T(2,128)}, u32[]{:S(2)}) copy-start(s32[2,128]{1,0:T(2,128)} %param.8) | copy-start | bytes 3076
  9.6 9.9 %copy-start.3 = (f32[2,2,128,128]{3,2,1,0:T(8,128)S(1)}, f32[2,2,128,128]{3,2,1,0:T(8,128)}, u32[]{:S(2)}) copy-start(f32[2,2,128,128]{3,2,1,0:T(8,128)} %param.6) | copy-start | bytes 786436
  9.6 44.5 %copy-start.5 = (s32[2]{0:T(128)S(1)}, s32[2]{0:T(128)}, u32[]{:S(2)}) copy-start(s32[2]{0:T(128)} %param.9) | copy-start | bytes 28
  9.6 44.6 %all-to-all-start = ((f32[32,2,128,64]{2,3,1,0:T(8,128)}), f32[32,2,128,64]{2,3,1,0:T(8,128)S(1)}, u32[]{:S(2)}, u32[]{:S(2)}) async-start(f32[32,2,128,64]{2,3,1,0:T(8,128)} %stack.14), calls=%async_computation | async-start | bytes 4194304 | tf_op jit(solution)/shard_map/all_to_all | solution.py:49
  19.3 121.6 %reduce-scatter.2.cloned.1.call-start = ((), (), s32[]{:S(2)}) async-start(), calls=%async_computation.2 | async-start | bytes 4456448 | tf_op jit(solution)/shard_map/reduce_scatter | solution.py:55
  54.4 1.0 copy-start.2
  65.1 171.4 %copy-start.1 = (f32[1,2,2048,128]{3,2,1,0:T(8,128)S(1)}, f32[1,2,2048,128]{3,2,1,0:T(8,128)}, u32[]{:S(2)}) copy-start(f32[1,2,2048,128]{3,2,1,0:T(8,128)} %param.11) | copy-start | bytes 6291460
  65.1 171.4 %all-gather.2.cloned.1.call-start = ((), (), s32[]{:S(2)}) async-start(), calls=%async_computation.3 | async-start | bytes 4456448 | tf_op jit(solution)/shard_map/all_gather | solution.py:56
  236.4 7.0 %copy-start = (f32[2,2,128,2048]{3,2,0,1:T(8,128)S(1)}, f32[2,2,128,2048]{3,2,0,1:T(8,128)}, u32[]{:S(2)}) copy-start(f32[2,2,128,2048]{3,2,0,1:T(8,128)} %all-gather.2.cloned.1.call-done) | copy-start | bytes 12582916
Sparse Core Ops, SparseCore 0:
  65.2 75.7 reduce-scatter.1
  143.0 93.4 all-gather.1
